TPU v7x, 32 devices: a whole 2x2x4 slice. The times are simulated.
32 devices in a mesh: dp: 2 (over core), row: 4 (over y, x), col: 4 (over z).
Axes of the slice: x: 2, y: 2, z: 4, core: 2. Of those that a mesh axis runs over, the one named last changes fastest.
Arguments:
- patches: bfloat16 [1536, 6144], P(('dp', 'col'), 'row'), may hold values from -250 to 250
- norm_gain: float32 [6144], P('row'), may hold values from 0.1 to 1.9
- w_in: bfloat16 [6144, 12288], P('row', 'col'), may hold values from -0.078125 to 0.078125
- w_out: bfloat16 [12288, 6144], P('col', 'row'), may hold values from -0.0546875 to 0.0546875
- out_grad: bfloat16 [1536, 6144], P(('dp', 'col'), 'row'), may hold values from -3 to 3
Outputs:
- branch: bfloat16 [1536, 6144], P(('dp', 'col'), 'row')
- grad_patches: bfloat16 [1536, 6144], P(('dp', 'col'), 'row')
- grad_w_in: float32 [6144, 12288], P('row', 'col')
- grad_w_out: float32 [12288, 6144], P('col', 'row')
- grad_gain: float32 [6144], P('row')
All inputs are finite; a program needn't handle non-finite values.
Results may differ from a plain program's by a relative error of at most 0.034.
Values may be sent and summed in bfloat16 or wider, within the bound.
A program may use at most 128 MiB of HBM per device.

v0:
```python
import jax
import jax.numpy as jnp
from jax import lax
from jax.sharding import PartitionSpec as P

D = 6144


def contract_tokens(left, right):
    return lax.dot_general(
        left, right, (((0,), (0,)), ((), ())), preferred_element_type=jnp.float32
    )


def contract_last(left, right):
    return lax.dot_general(
        left, right, (((1,), (1,)), ((), ())), preferred_element_type=jnp.float32
    )


def statistics(values):
    return (jnp.sum(values, axis=1), jnp.sum(values * values, axis=1))


def finish_norm(values, sums, squares):
    average = (sums / D)[:, None]
    inverse = lax.rsqrt((squares / D)[:, None] - average * average + 1e-06)
    return ((values - average) * inverse, inverse)


def shards(patches, norm_gain, w_in, w_out, out_grad):
    values = patches.astype(jnp.float32)
    sums, squares = lax.psum(statistics(values), "row")
    centred, inverse = finish_norm(values, sums, squares)
    normed_panel = lax.all_gather(
        (centred * norm_gain).astype(jnp.bfloat16), "col", axis=0, tiled=True
    )
    picked = normed_panel
    pre = lax.psum_scatter(
        jnp.dot(picked, w_in, preferred_element_type=jnp.float32).astype(jnp.bfloat16),
        "row",
        scatter_dimension=0,
        tiled=True,
    ).astype(jnp.float32)
    activation, slope = jax.vjp(jax.nn.gelu, pre)
    hidden_panel = lax.all_gather(activation.astype(jnp.bfloat16), "row", axis=0, tiled=True)
    picked = hidden_panel
    branch = lax.psum_scatter(
        jnp.dot(picked, w_out, preferred_element_type=jnp.float32).astype(jnp.bfloat16),
        "col",
        scatter_dimension=0,
        tiled=True,
    )
    cotangent = lax.all_gather(out_grad, "col", axis=0, tiled=True)
    picked = cotangent
    hid_grad = lax.psum_scatter(
        contract_last(picked, w_out).astype(jnp.bfloat16), "row", scatter_dimension=0, tiled=True
    ).astype(jnp.float32)
    pre_grad = lax.all_gather(slope(hid_grad)[0].astype(jnp.bfloat16), "row", axis=0, tiled=True)
    picked = pre_grad
    normed_grad = lax.psum_scatter(
        contract_last(picked, w_in).astype(jnp.bfloat16), "col", scatter_dimension=0, tiled=True
    ).astype(jnp.float32)
    local_in = contract_tokens(normed_panel, pre_grad).astype(jnp.bfloat16)
    local_out = contract_tokens(hidden_panel, cotangent).astype(jnp.bfloat16)
    grad_w_in, grad_w_out = (
        lax.psum(local_in, "dp").astype(jnp.float32),
        lax.psum(local_out, "dp").astype(jnp.float32),
    )
    grad_gain = lax.psum(jnp.sum(normed_grad * centred, axis=0), ("dp", "col"))
    scaled = normed_grad * norm_gain
    first, second = lax.psum((jnp.sum(scaled, axis=1), jnp.sum(scaled * centred, axis=1)), "row")
    grad_patches = inverse * (scaled - (first / D)[:, None] - centred * (second / D)[:, None])
    return (branch, grad_patches.astype(jnp.bfloat16), grad_w_in, grad_w_out, grad_gain)


def solution(mesh):
    return jax.shard_map(
        shards,
        mesh=mesh,
        in_specs=(
            P(("dp", "col"), "row"),
            P("row"),
            P("row", "col"),
            P("col", "row"),
            P(("dp", "col"), "row"),
        ),
        out_specs=(
            P(("dp", "col"), "row"),
            P(("dp", "col"), "row"),
            P("row", "col"),
            P("col", "row"),
            P("row"),
        ),
        check_vma=False,
    )
```

profile of v0, /device:TPU:0, one launch (start us, length us, event | category | flops | bytes accessed | tf_op | source)
XLA Modules:
  0.0 540.4 jit_solution(461828414355947713)
XLA Ops:
  7.2 0.0 all-gather.5.cloned.1.call-start
  7.2 1.3 convert_reduce_fusion
  8.6 11.4 %all-reduce.1 = (f32[192]{0:T(256)S(1)}, f32[192]{0:T(256)S(1)}) all-reduce(f32[192]{0:T(256)S(1)} %get-tuple-element.9, f32[192]{0:T(256)S(1)} %get-tuple-element.8), channel_id=1, replica_groups=mesh['dp'=2,'row'=4,'col'=4] {'row'}, use_global_device_ids=true, to_apply=%region_3.0 | all-reduce | flops 384 | bytes 3072 | tf_op jit(solution)/shard_map/psum | solution.py:33
  19.9 2.3 fusion.22
  22.2 0.0 all-gather.5.cloned.1.call-update
  22.2 0.0 all-gather.9.cloned.1.call-start
  22.3 0.7 all-gather.9.cloned.1.call-update
  23.0 0.0 reduce-scatter.5.cloned.1.call-start
  23.0 49.2 %all-gather.5.cloned.1.call-done = bf16[768,1536]{1,0:T(8,128)(2,1)} async-done(((bf16[192,1536]{1,0:T(8,128)(2,1)}), bf16[768,1536]{1,0:T(8,128)(2,1)}) %all-gather.5.cloned.1.call-update) | async-done | bytes 2359312 | tf_op jit(solution)/shard_map/all_gather | solution.py:35
  72.2 12.1 %convolution_convert_fusion.3 = bf16[768,3072]{1,0:T(8,128)(2,1)} fusion(bf16[768,1536]{1,0:T(8,128)(2,1)} %all-gather.5.cloned.1.call-done, bf16[1536,3072]{1,0:T(8,128)(2,1)} %param.7), kind=kOutput, calls=%fused_computation.3 | convolution fusion | flops 7250116608 | bytes 16515072 | tf_op jit(solution)/shard_map/dot_general | solution.py:40
  84.4 0.0 reduce-scatter.5.cloned.1.call-update
  84.4 0.0 reduce-scatter.9.cloned.1.call-start
  84.5 38.7 %all-gather.9.cloned.1.call-done = bf16[768,1536]{1,0:T(8,128)(2,1)} async-done(((bf16[192,1536]{1,0:T(8,128)(2,1)}), bf16[768,1536]{1,0:T(8,128)(2,1)}) %all-gather.9.cloned.1.call-update) | async-done | bytes 2359312 | tf_op jit(solution)/shard_map/all_gather | solution.py:54
  123.1 12.2 %convolution_convert_fusion.2 = bf16[768,3072]{1,0:T(8,128)(2,1)} fusion(bf16[768,1536]{1,0:T(8,128)(2,1)} %all-gather.9.cloned.1.call-done, bf16[3072,1536]{1,0:T(8,128)(2,1)} %param.8), kind=kOutput, calls=%fused_computation.2 | convolution fusion | flops 7250116608 | bytes 16515072 | tf_op jit(solution)/shard_map/dot_general | solution.py:16
  135.4 0.0 reduce-scatter.9.cloned.1.call-update
  135.4 0.0 all-gather.11.cloned.1.call-start
  135.4 47.2 %reduce-scatter.5.cloned.1.call-done = bf16[192,3072]{1,0:T(8,128)(2,1)} async-done(((bf16[768,3072]{1,0:T(8,128)(2,1)}), bf16[192,3072]{1,0:T(8,128)(2,1)}) %reduce-scatter.5.cloned.1.call-update) | async-done | bytes 1179664 | tf_op jit(solution)/shard_map/reduce_scatter | solution.py:39
  182.6 60.6 %reduce-scatter.9.cloned.1.call-done = bf16[192,3072]{1,0:T(8,128)(2,1)} async-done(((bf16[768,3072]{1,0:T(8,128)(2,1)}), bf16[192,3072]{1,0:T(8,128)(2,1)}) %reduce-scatter.9.cloned.1.call-update) | async-done | bytes 1179664 | tf_op jit(solution)/shard_map/reduce_scatter | solution.py:56
  243.2 4.9 fusion.3
  248.1 0.0 all-gather.11.cloned.1.call-update
  248.1 0.0 all-gather.7.cloned.1.call-start
  248.1 0.5 all-gather.7.cloned.1.call-update
  248.7 0.0 reduce-scatter.11.cloned.1.call-start
  248.7 56.6 %all-gather.11.cloned.1.call-done = bf16[768,3072]{1,0:T(8,128)(2,1)} async-done(((bf16[192,3072]{1,0:T(8,128)(2,1)}), bf16[768,3072]{1,0:T(8,128)(2,1)}) %all-gather.11.cloned.1.call-update) | async-done | bytes 4718608 | tf_op jit(solution)/shard_map/all_gather | solution.py:59
  305.3 12.6 %convolution_convert_fusion.4 = bf16[768,1536]{1,0:T(8,128)(2,1)} fusion(bf16[768,3072]{1,0:T(8,128)(2,1)} %all-gather.11.cloned.1.call-done, bf16[1536,3072]{1,0:T(8,128)(2,1)} %param.7), kind=kOutput, calls=%fused_computation.10 | convolution fusion | flops 7248936960 | bytes 16515072 | tf_op jit(solution)/shard_map/dot_general | solution.py:16
  317.9 0.0 copy-start.2
  317.9 0.0 reduce-scatter.11.cloned.1.call-update
  317.9 0.2 all-reduce.5.cloned.1.call-start
  318.2 1.4 copy-done.2
  319.6 12.0 %convolution_convert_fusion.1 = bf16[1536,3072]{1,0:T(8,128)(2,1)} fusion(bf16[768,1536]{1,0:T(8,128)(2,1)S(1)} %copy-done.2, bf16[768,3072]{1,0:T(8,128)(2,1)} %all-gather.11.cloned.1.call-done), kind=kOutput, calls=%fused_computation.1 | convolution fusion | flops 7252475904 | bytes 16515072 | tf_op jit(solution)/shard_map/dot_general | solution.py:10
  331.5 33.2 %all-gather.7.cloned.1.call-done = bf16[768,3072]{1,0:T(8,128)(2,1)} async-done(((bf16[192,3072]{1,0:T(8,128)(2,1)}), bf16[768,3072]{1,0:T(8,128)(2,1)}) %all-gather.7.cloned.1.call-update) | async-done | bytes 4718608 | tf_op jit(solution)/shard_map/all_gather | solution.py:46
  364.7 12.3 %convolution_convert_fusion = bf16[3072,1536]{1,0:T(8,128)(2,1)} fusion(bf16[768,3072]{1,0:T(8,128)(2,1)} %all-gather.7.cloned.1.call-done, bf16[768,1536]{1,0:T(8,128)(2,1)} %all-gather.9.cloned.1.call-done), kind=kOutput, calls=%fused_computation | convolution fusion | flops 7252475904 | bytes 16515072 | tf_op jit(solution)/shard_map/dot_general | solution.py:10
  377.0 0.0 all-reduce.5.cloned.1.call-update
  377.1 0.0 reduce-scatter.7.cloned.1.call-start
  377.1 12.6 %convolution_convert_fusion.5 = bf16[768,1536]{1,0:T(8,128)(2,1)} fusion(bf16[768,3072]{1,0:T(8,128)(2,1)} %all-gather.7.cloned.1.call-done, bf16[3072,1536]{1,0:T(8,128)(2,1)} %param.8), kind=kOutput, calls=%fused_computation.11 | convolution fusion | flops 7248936960 | bytes 16515072 | tf_op jit(solution)/shard_map/dot_general | solution.py:49
  389.7 0.0 copy-start
  389.7 0.0 copy-start.1
  389.7 0.0 reduce-scatter.7.cloned.1.call-update
  389.7 25.3 %reduce-scatter.11.cloned.1.call-done = bf16[192,1536]{1,0:T(8,128)(2,1)} async-done(((bf16[768,1536]{1,0:T(8,128)(2,1)}), bf16[192,1536]{1,0:T(8,128)(2,1)}) %reduce-scatter.11.cloned.1.call-update) | async-done | bytes 589840 | tf_op jit(solution)/shard_map/reduce_scatter | solution.py:61
  415.1 0.0 copy-done
  415.1 0.0 copy-done.1
  415.1 1.7 fusion.18
  416.7 9.9 %all-reduce = (f32[192]{0:T(256)S(1)}, f32[192]{0:T(256)S(1)}) all-reduce(f32[192]{0:T(256)S(1)} %get-tuple-element.6, f32[192]{0:T(256)S(1)} %get-tuple-element.7), channel_id=1, replica_groups=mesh['dp'=2,'row'=4,'col'=4] {'row'}, use_global_device_ids=true, to_apply=%region_11.0 | all-reduce | flops 384 | bytes 3072 | tf_op jit(solution)/shard_map/psum | solution.py:72
  426.6 15.2 %psum.55 = f32[1536]{0:T(1024)} all-reduce(f32[1536]{0:T(1024)S(1)} %get-tuple-element.5), channel_id=1, replica_groups=mesh['dp'=2,'row'=4,'col'=4] {'dp','col'}, use_global_device_ids=true, to_apply=%region_15.0 | all-reduce | flops 1536 | bytes 12288 | tf_op jit(solution)/shard_map/psum | solution.py:70
  441.8 2.5 fusion.16
  444.3 37.2 %all-reduce.5.cloned.1.call-done = (bf16[1536,3072]{1,0:T(8,128)(2,1)}, bf16[3072,1536]{1,0:T(8,128)(2,1)}) async-done(((bf16[1536,3072]{1,0:T(8,128)(2,1)}, bf16[3072,1536]{1,0:T(8,128)(2,1)}), (bf16[1536,3072]{1,0:T(8,128)(2,1)}, bf16[3072,1536]{1,0:T(8,128)(2,1)})) %all-reduce.5.cloned.1.call-update) | async-done | bytes 18874384 | tf_op jit(solution)/shard_map/psum | solution.py:67
  481.5 12.7 %convert_element_type.61 = f32[1536,3072]{1,0:T(8,128)} convert(bf16[1536,3072]{1,0:T(8,128)(2,1)} %get-tuple-element.14) | non-fusion elementwise | flops 4718592 | bytes 28311552 | tf_op jit(solution)/shard_map/convert_element_type | solution.py:67
  494.2 13.2 %convert_element_type.63 = f32[3072,1536]{1,0:T(8,128)} convert(bf16[3072,1536]{1,0:T(8,128)(2,1)} %get-tuple-element.15) | non-fusion elementwise | flops 4718592 | bytes 28311552 | tf_op jit(solution)/shard_map/convert_element_type | solution.py:68
  507.4 26.4 %reduce-scatter.7.cloned.1.call-done = bf16[192,1536]{1,0:T(8,128)(2,1)} async-done(((bf16[768,1536]{1,0:T(8,128)(2,1)}), bf16[192,1536]{1,0:T(8,128)(2,1)}) %reduce-scatter.7.cloned.1.call-update) | async-done | bytes 589840 | tf_op jit(solution)/shard_map/reduce_scatter | solution.py:48
  (2 shorter events, 0.0 us)
Async XLA Ops:
  7.2 65.1 %all-gather.5.cloned.1.call-start = ((), (), s32[]{:S(2)}) async-start(), calls=%async_computation.4 | async-start | bytes 2949120 | tf_op jit(solution)/shard_map/all_gather | solution.py:35
  22.2 100.9 %all-gather.9.cloned.1.call-start = ((), (), s32[]{:S(2)}) async-start(), calls=%async_computation.8 | async-start | bytes 2949120 | tf_op jit(solution)/shard_map/all_gather | solution.py:54
  23.0 159.7 %reduce-scatter.5.cloned.1.call-start = ((), (), s32[]{:S(2)}) async-start(), calls=%async_computation.5 | async-start | bytes 5898240 | tf_op jit(solution)/shard_map/reduce_scatter | solution.py:39
  84.4 158.8 %reduce-scatter.9.cloned.1.call-start = ((), (), s32[]{:S(2)}) async-start(), calls=%async_computation.9 | async-start | bytes 5898240 | tf_op jit(solution)/shard_map/reduce_scatter | solution.py:56
  135.4 170.0 %all-gather.11.cloned.1.call-start = ((), (), s32[]{:S(2)}) async-start(), calls=%async_computation.10 | async-start | bytes 5898240 | tf_op jit(solution)/shard_map/all_gather | solution.py:59
  248.1 116.6 %all-gather.7.cloned.1.call-start = ((), (), s32[]{:S(2)}) async-start(), calls=%async_computation.6 | async-start | bytes 5898240 | tf_op jit(solution)/shard_map/all_gather | solution.py:46
  248.7 166.4 %reduce-scatter.11.cloned.1.call-start = ((), (), s32[]{:S(2)}) async-start(), calls=%async_computation.11 | async-start | bytes 2949120 | tf_op jit(solution)/shard_map/reduce_scatter | solution.py:61
  317.9 1.7 copy-start.2
  317.9 163.6 %all-reduce.5.cloned.1.call-start = ((), (), s32[]{:S(2)}) async-start(), calls=%async_computation.12 | async-start | bytes 37748736 | tf_op jit(solution)/shard_map/psum | solution.py:67
  377.1 156.8 %reduce-scatter.7.cloned.1.call-start = ((), (), s32[]{:S(2)}) async-start(), calls=%async_computation.7 | async-start | bytes 2949120 | tf_op jit(solution)/shard_map/reduce_scatter | solution.py:48
  389.7 25.4 %copy-start = (bf16[192,1536]{1,0:T(8,128)(2,1)S(1)}, bf16[192,1536]{1,0:T(8,128)(2,1)}, u32[]{:S(2)}) copy-start(bf16[192,1536]{1,0:T(8,128)(2,1)} %param.5) | copy-start | bytes 1769476
  389.7 25.4 %copy-start.1 = (f32[1536]{0:T(1024)S(1)}, f32[1536]{0:T(1024)}, u32[]{:S(2)}) copy-start(f32[1536]{0:T(1024)} %param.6) | copy-start | bytes 18436
Sparse Core Ops, SparseCore 0:
  22.3 49.8 all-gather.4
  73.8 49.2 all-gather.8
  126.7 55.8 reduce-scatter.4
  186.0 57.0 reduce-scatter.8
  248.2 57.0 all-gather.10
  307.6 57.0 all-gather.6
  367.0 48.0 reduce-scatter.10
  418.2 63.2 all-reduce.4
  484.5 49.3 reduce-scatter.6
where the time goes:
time: 541 us; the launch traced here: 540 us
  waiting for transfers between devices  376 us (70%)
  matrix products  73.8 us (14%)
  other arithmetic  38.7 us (7%)
  blocking collectives  36.4 us (7%)
  between operations  13.9 us (3%)
    reduce_scatter x1, waiting for transfers between devices, shards(): lax.psum_scatter(contract_last(picked, w_out).astype(jnp.bfloat16), 'row'...  60.6 us
    all_gather x1, waiting for transfers between devices, shards(): lax.all_gather(slope(hid_grad)[0].astype(jnp.bfloat16), 'row', axis=0, ti...  56.6 us
    all_gather x1, waiting for transfers between devices, shards(): lax.all_gather((centred * norm_gain).astype(jnp.bfloat16), 'col', axis=0,...  49.2 us
    reduce_scatter x1, waiting for transfers between devices, shards(): lax.psum_scatter(jnp.dot(picked, w_in, preferred_element_type=jnp.float32...  47.2 us
    all_gather x1, waiting for transfers between devices, shards(): cotangent = lax.all_gather(out_grad, 'col', axis=0, tiled=True)  38.7 us
    psum x1, waiting for transfers between devices, shards(): lax.psum(local_in, 'dp').astype(jnp.float32)  37.2 us
    all_gather x1, waiting for transfers between devices, shards(): lax.all_gather(activation.astype(jnp.bfloat16), 'row', axis=0, tiled=True)  33.2 us
    reduce_scatter x1, waiting for transfers between devices, shards(): lax.psum_scatter(jnp.dot(picked, w_out, preferred_element_type=jnp.float3...  26.4 us
  transfers between devices with their start and end apart: 9, of which 9 were waited for; matrix products, arithmetic and copies ran while one was open for 19% of the time, Pallas kernels for 0%

commit v1 on v0

v1 whole, which is shorter than its diff:
```python
import functools

import jax
import jax.numpy as jnp
from jax import lax
from jax.experimental import pallas as pl
from jax.experimental.pallas import tpu as pltpu
from jax.sharding import PartitionSpec as P

D = 6144
MESH = pl.DeviceIdType.MESH
F32 = jnp.float32
BF16 = jnp.bfloat16

COT, NRM, HG, PRE, HID, PG, BR, NG, ST1, ST2, GG = range(11)


def flip(i, k, n):
    total, bit = 0, 1
    while bit < n:
        k_bit = (k // bit) % 2 if isinstance(k, int) else lax.rem(lax.div(k, jnp.int32(bit)), jnp.int32(2))
        i_bit = lax.rem(lax.div(i, jnp.int32(bit)), jnp.int32(2))
        total = total + lax.rem(i_bit + k_bit, jnp.int32(2)) * bit
        bit *= 2
    return total


def dot(left, right, left_dim=1, right_dim=0):
    return lax.dot_general(left, right, (((left_dim,), (right_dim,)), ((), ())), preferred_element_type=F32)


def gelu_and_slope(x):
    a, b = 0.7978845608028654, 0.044715
    square = x * x
    t = jnp.tanh(a * (x + b * (square * x)))
    half = 0.5 * (1.0 + t)
    return x * half, half + 0.5 * x * (1.0 - t * t) * (a * (1.0 + 3.0 * b * square))


def kernel(
    n, patches, gain, w_in, w_out, out_grad,
    branch, grad_patches, gwi, gwo, ggain,
    wi, wo, cot, nrm, hid, pg, rhg, rpre, stage, rbr, rng, st1, st2, ggr, ggd, lhs, dstage, drecv, obuf,
    wsem, send, recv, dsend, drsem, osem, ggsem, credit,
):
    tb, dl = patches.shape
    fl = w_in.shape[1]
    wf = 256 if fl % 256 == 0 else 128
    wd = 256 if dl % 256 == 0 else 128
    tile = dstage.shape[1]
    r, c, d = lax.axis_index("row"), lax.axis_index("col"), lax.axis_index("dp")

    def rows(j):
        return pl.ds(pl.multiple_of(j * tb, tb), tb)

    def cols(t, width, start=0):
        return pl.ds(pl.multiple_of(start + t * width, width), width)

    load_out = pltpu.make_async_copy(w_out, wo, wsem.at[0])
    load_in = pltpu.make_async_copy(w_in, wi, wsem.at[1])
    load_out.start()
    load_in.start()

    barrier = pltpu.get_barrier_semaphore()
    for k in range(1, n):
        pl.semaphore_signal(barrier, inc=1, device_id={"row": flip(r, k, n)}, device_id_type=MESH)
        pl.semaphore_signal(barrier, inc=1, device_id={"col": flip(c, k, n)}, device_id_type=MESH)
    pl.semaphore_signal(barrier, inc=1, device_id={"dp": 1 - d}, device_id_type=MESH)
    pl.semaphore_wait(barrier, 2 * (n - 1) + 1)

    def copy(kind, src, dst, send_at, recv_at, axis, peer):
        return pltpu.make_async_remote_copy(
            src_ref=src, dst_ref=dst, send_sem=send.at[kind, send_at], recv_sem=recv.at[kind, recv_at],
            device_id={axis: peer}, device_id_type=MESH,
        )

    def cot_copy(k):
        return copy(COT, out_grad, cot.at[rows(c)], k, c, "col", flip(c, k, n))

    def nrm_copy(k):
        return copy(NRM, nrm.at[rows(c)], nrm.at[rows(c)], k, c, "col", flip(c, k, n))

    def hid_copy(k):
        return copy(HID, hid.at[rows(r)], hid.at[rows(r)], k, r, "row", flip(r, k, n))

    def pg_copy(k):
        return copy(PG, pg.at[rows(r)], pg.at[rows(r)], k, r, "row", flip(r, k, n))

    def arrival(kind, ref, source, axis):
        copy(kind, ref, ref, 0, source, axis, source).wait_recv()

    for k in range(1, n):
        cot_copy(k).start()
    cot[rows(c), :] = out_grad[...]

    values = patches[...].astype(F32)
    lane = lax.broadcasted_iota(jnp.int32, (tb, 128), 1)
    st1[r] = jnp.where(
        lane == 0, jnp.sum(values, axis=1, keepdims=True), jnp.sum(values * values, axis=1, keepdims=True)
    )
    for k in range(1, n):
        copy(ST1, st1.at[r], st1.at[r], k, r, "row", flip(r, k, n)).start()

    def hg_copy(kind, dst, j):
        return copy(kind, stage.at[j], dst.at[r], j, r, "row", j)

    def scatter_row(kind, k, panel, product, dst):
        j = flip(c, k, n)
        mine = j == r

        if kind == PRE:
            @pl.when(jnp.logical_not(mine))
            def _():
                hg_copy(HG, rhg, j).wait_send()

        def body(t, carry):
            term = product(panel[rows(j), :], t).astype(BF16)

            @pl.when(mine)
            def _():
                dst[r, :, cols(t, wf)] = term

            @pl.when(jnp.logical_not(mine))
            def _():
                stage[j, :, cols(t, wf)] = term

            return carry

        lax.fori_loop(0, fl // wf, body, 0)

        @pl.when(jnp.logical_not(mine))
        def _():
            hg_copy(kind, dst, j).start()

    def hg_product(left, t):
        return dot(left, wo[cols(t, wf), :], 1, 1)

    def pre_product(left, t):
        return dot(left, wi[:, cols(t, wf)])

    load_out.wait()
    scatter_row(HG, jnp.int32(0), cot, hg_product, rhg)

    for k in range(1, n):
        arrival(ST1, st1.at[flip(r, k, n)], flip(r, k, n), "row")
    sums = st1[0]
    for q in range(1, n):
        sums = sums + st1[q]
    average = sums[:, 0:1] / D
    inverse = lax.rsqrt(sums[:, 1:2] / D - average * average + 1e-06)
    nrm[rows(c), :] = ((patches[...].astype(F32) - average) * inverse * gain[...]).astype(BF16)

    def hg_step(k, carry):
        source = flip(c, k, n)
        arrival(COT, cot.at[rows(source)], source, "col")
        cot_copy(k).wait_send()
        nrm_copy(k).start()
        scatter_row(HG, k, cot, hg_product, rhg)
        return carry

    lax.fori_loop(1, n, hg_step, 0)
    load_in.wait()

    def pre_step(k, carry):
        source = flip(c, k, n)

        @pl.when(k > 0)
        def _():
            arrival(NRM, nrm.at[rows(source)], source, "col")
            nrm_copy(k).wait_send()

        scatter_row(PRE, k, nrm, pre_product, rpre)
        return carry

    lax.fori_loop(0, n, pre_step, 0)

    for k in range(1, n):
        source = flip(r, k, n)
        arrival(HG, rhg.at[source], source, "row")
        arrival(PRE, rpre.at[source], source, "row")

    def hidden_step(t, carry):
        at = cols(t, wf)
        pre, grad = rpre[0, :, at].astype(F32), rhg[0, :, at].astype(F32)
        for q in range(1, n):
            pre = pre + rpre[q, :, at].astype(F32)
            grad = grad + rhg[q, :, at].astype(F32)
        activation, slope = gelu_and_slope(pre)
        hid[rows(r), at] = activation.astype(BF16)
        pg[rows(r), at] = (grad * slope).astype(BF16)
        return carry

    lax.fori_loop(0, fl // wf, hidden_step, 0)
    for k in range(1, n):
        hid_copy(k).start()
    for k in range(1, n):
        hg_copy(PRE, rpre, flip(r, k, n)).wait_send()

    def br_copy(kind, dst, j, start):
        return copy(kind, stage.at[j, :, pl.ds(start, dl)], dst.at[c], j, c, "col", j)

    def scatter_col(kind, k, panel, product, dst, start):
        j = flip(r, k, n)
        mine = j == c

        def body(t, carry):
            term = product(panel[rows(j), :], t).astype(BF16)

            @pl.when(mine)
            def _():
                dst[c, :, cols(t, wd)] = term

            @pl.when(jnp.logical_not(mine))
            def _():
                stage[j, :, cols(t, wd, start)] = term

            return carry

        lax.fori_loop(0, dl // wd, body, 0)

        @pl.when(jnp.logical_not(mine))
        def _():
            br_copy(kind, dst, j, start).start()

    def branch_step(k, carry):
        source = flip(r, k, n)

        @pl.when(k > 0)
        def _():
            arrival(HID, hid.at[rows(source)], source, "row")
            hid_copy(k).wait_send()
            pg_copy(k).start()

        scatter_col(BR, k, hid, lambda left, t: dot(left, wo[:, cols(t, wd)]), rbr, 0)
        return carry

    lax.fori_loop(0, n, branch_step, 0)

    def tile_copy(slot):
        return pltpu.make_async_remote_copy(
            src_ref=dstage.at[slot], dst_ref=drecv.at[slot], send_sem=dsend.at[slot], recv_sem=drsem.at[slot],
            device_id={"dp": 1 - d}, device_id_type=MESH,
        )

    def weight_grad(left, right, out, per_row, first, last):
        count = (out.shape[0] // tile) * per_row

        def place(t):
            if per_row == 1:
                return out.at[cols(t, tile), :]
            return out.at[cols(lax.div(t, jnp.int32(per_row)), tile), cols(lax.rem(t, jnp.int32(per_row)), dl)]

        def result_copy(t):
            slot = lax.rem(t, jnp.int32(2))
            return pltpu.make_async_copy(obuf.at[slot], place(t), osem.at[slot])

        def finish(t):
            slot = lax.rem(t, jnp.int32(2))
            tile_copy(slot).wait_send()
            tile_copy(slot).wait_recv()

            @pl.when(t >= 2)
            def _():
                result_copy(t - 2).wait()

            obuf[slot] = (dstage[slot].astype(F32) + drecv[slot].astype(F32)).astype(BF16)
            result_copy(t).start()

            def free():
                pl.semaphore_signal(credit, inc=1, device_id={"dp": 1 - d}, device_id_type=MESH)

            if last:
                pl.when(t < count - 2)(free)
            else:
                free()

        def step(t, carry):
            slot = lax.rem(t, jnp.int32(2))
            lhs[...] = left[:, cols(lax.div(t, jnp.int32(per_row)), tile)].T
            shift = lax.rem(t, jnp.int32(per_row)) * dl

            def part(p, inner):
                dstage[slot, :, cols(p, wd)] = dot(
                    lhs[...], right[:, pl.ds(pl.multiple_of(shift + p * wd, wd), wd)]
                ).astype(BF16)
                return inner

            lax.fori_loop(0, dl // wd, part, 0)

            def claim():
                pl.semaphore_wait(credit, 1)

            if first:
                pl.when(t >= 2)(claim)
            else:
                claim()
            tile_copy(slot).start()

            @pl.when(t >= 1)
            def _():
                finish(t - 1)

            return carry

        lax.fori_loop(0, count, step, 0)
        finish(jnp.int32(count - 1))
        result_copy(jnp.int32(count - 2)).wait()
        result_copy(jnp.int32(count - 1)).wait()

    weight_grad(hid, cot, gwo, 1, True, False)

    def ng_step(k, carry):
        source = flip(r, k, n)

        @pl.when(k > 0)
        def _():
            arrival(PG, pg.at[rows(source)], source, "row")
            pg_copy(k).wait_send()

        scatter_col(NG, k, pg, lambda left, t: dot(left, wi[cols(t, wd), :], 1, 1), rng, dl)
        return carry

    lax.fori_loop(0, n, ng_step, 0)
    weight_grad(nrm, pg, gwi, fl // dl, False, True)

    for k in range(1, n):
        arrival(NG, rng.at[flip(c, k, n)], flip(c, k, n), "col")
    total = rng[0].astype(F32)
    for q in range(1, n):
        total = total + rng[q].astype(F32)
    centred = (patches[...].astype(F32) - average) * inverse
    weighted = total * centred
    ggr[c] = jnp.broadcast_to(jnp.sum(weighted, axis=0, keepdims=True), (8, dl))
    scaled = total * gain[...]
    st2[r] = jnp.where(
        lane == 0, jnp.sum(scaled, axis=1, keepdims=True),
        jnp.sum(weighted * gain[...], axis=1, keepdims=True),
    )
    for k in range(1, n):
        copy(ST2, st2.at[r], st2.at[r], k, r, "row", flip(r, k, n)).start()
        copy(GG, ggr.at[c], ggr.at[c], k, c, "col", flip(c, k, n)).start()
    for k in range(1, n):
        arrival(BR, rbr.at[flip(c, k, n)], flip(c, k, n), "col")
    out = rbr[0].astype(F32)
    for q in range(1, n):
        out = out + rbr[q].astype(F32)
    branch[...] = out.astype(BF16)

    for k in range(1, n):
        arrival(GG, ggr.at[flip(c, k, n)], flip(c, k, n), "col")
    own = ggr[0]
    for q in range(1, n):
        own = own + ggr[q]
    ggd[0] = own
    gain_copy = pltpu.make_async_remote_copy(
        src_ref=ggd.at[0], dst_ref=ggd.at[1], send_sem=ggsem.at[0], recv_sem=ggsem.at[1],
        device_id={"dp": 1 - d}, device_id_type=MESH,
    )
    gain_copy.start()
    for k in range(1, n):
        arrival(ST2, st2.at[flip(r, k, n)], flip(r, k, n), "row")
    sums = st2[0]
    for q in range(1, n):
        sums = sums + st2[q]
    first, second = sums[:, 0:1] / D, sums[:, 1:2] / D
    total = rng[0].astype(F32)
    for q in range(1, n):
        total = total + rng[q].astype(F32)
    centred = (patches[...].astype(F32) - average) * inverse
    grad_patches[...] = (inverse * (total * gain[...] - first - centred * second)).astype(BF16)
    gain_copy.wait()
    ggain[...] = ggd[0] + ggd[1]

    for k in range(1, n):
        copy(ST1, st1.at[r], st1.at[r], k, r, "row", flip(r, k, n)).wait_send()
        copy(ST2, st2.at[r], st2.at[r], k, r, "row", flip(r, k, n)).wait_send()
        copy(GG, ggr.at[c], ggr.at[c], k, c, "col", flip(c, k, n)).wait_send()
        br_copy(BR, rbr, flip(c, k, n), 0).wait_send()
        br_copy(NG, rng, flip(c, k, n), dl).wait_send()


def shards(n, patches, norm_gain, w_in, w_out, out_grad):
    tb, dl = patches.shape
    fl = w_in.shape[1]
    tile = 256 if dl % 256 == 0 and fl % 256 == 0 else 128
    vmem = pl.BlockSpec(memory_space=pltpu.VMEM)
    hbm = pl.BlockSpec(memory_space=pl.ANY)
    out = jax.ShapeDtypeStruct
    flops = 12 * n * tb * dl * fl
    branch, grad_patches, gwi, gwo, ggain = pl.pallas_call(
        functools.partial(kernel, n),
        out_shape=(
            out((tb, dl), BF16), out((tb, dl), BF16), out((dl, fl), BF16), out((fl, dl), BF16), out((8, dl), F32),
        ),
        in_specs=[vmem, vmem, hbm, hbm, vmem],
        out_specs=(vmem, vmem, hbm, hbm, vmem),
        scratch_shapes=[
            pltpu.VMEM((dl, fl), BF16),
            pltpu.VMEM((fl, dl), BF16),
            pltpu.VMEM((n * tb, dl), BF16),
            pltpu.VMEM((n * tb, dl), BF16),
            pltpu.VMEM((n * tb, fl), BF16),
            pltpu.VMEM((n * tb, fl), BF16),
            pltpu.VMEM((n, tb, fl), BF16),
            pltpu.VMEM((n, tb, fl), BF16),
            pltpu.VMEM((n, tb, fl), BF16),
            pltpu.VMEM((n, tb, dl), BF16),
            pltpu.VMEM((n, tb, dl), BF16),
            pltpu.VMEM((n, tb, 128), F32),
            pltpu.VMEM((n, tb, 128), F32),
            pltpu.VMEM((n, 8, dl), F32),
            pltpu.VMEM((2, 8, dl), F32),
            pltpu.VMEM((tile, n * tb), BF16),
            pltpu.VMEM((2, tile, dl), BF16),
            pltpu.VMEM((2, tile, dl), BF16),
            pltpu.VMEM((2, tile, dl), BF16),
            pltpu.SemaphoreType.DMA((2,)),
            pltpu.SemaphoreType.DMA((11, n)),
            pltpu.SemaphoreType.DMA((11, n)),
            pltpu.SemaphoreType.DMA((2,)),
            pltpu.SemaphoreType.DMA((2,)),
            pltpu.SemaphoreType.DMA((2,)),
            pltpu.SemaphoreType.DMA((2,)),
            pltpu.SemaphoreType.REGULAR,
        ],
        compiler_params=pltpu.CompilerParams(
            collective_id=0, has_side_effects=True, vmem_limit_bytes=63 * 1024 * 1024
        ),
        cost_estimate=pl.CostEstimate(flops=flops, bytes_accessed=8 * dl * fl, transcendentals=tb * fl),
    )(patches, norm_gain.reshape(1, dl), w_in, w_out, out_grad)
    return branch, grad_patches, gwi.astype(F32), gwo.astype(F32), ggain[0]


def solution(mesh):
    n = mesh.shape["row"]
    if mesh.shape["col"] != n or mesh.shape["dp"] != 2 or n & (n - 1):
        raise ValueError("unsupported mesh")
    return jax.shard_map(
        functools.partial(shards, n),
        mesh=mesh,
        in_specs=(
            P(("dp", "col"), "row"),
            P("row"),
            P("row", "col"),
            P("col", "row"),
            P(("dp", "col"), "row"),
        ),
        out_specs=(
            P(("dp", "col"), "row"),
            P(("dp", "col"), "row"),
            P("row", "col"),
            P("col", "row"),
            P("row"),
        ),
        check_vma=False,
    )
```

time: 541 us -> 371 us (0.69)
  waiting for transfers between devices: 376 us -> 0 us
  Pallas kernels: 0 us -> 340 us
  matrix products: 73.8 us -> 0 us
  blocking collectives: 36.4 us -> 0 us
  between operations: 13.9 us -> 0.64 us
  other arithmetic: 38.7 us -> 26 us
    pallas_call x0 -> x1, Pallas kernels: none -> 340 us  [shards(): pl.pallas_call(functools.partial(kernel, n), out_shape=(out((tb, dl), BF1...]
    all_gather x4 -> x0, waiting for transfers between devices: 178 us -> none  [the longest x1 56.6 us: shards(): lax.all_gather(slope(hid_grad)[0].astype(jnp.bfloat16), 'row', axis=0, ti...]
    reduce_scatter x4 -> x0, waiting for transfers between devices: 160 us -> none  [the longest x1 60.6 us: shards(): lax.psum_scatter(contract_last(picked, w_out).astype(jnp.bfloat16), 'row'...]
    dot_general x6 -> x0, matrix products: 73.8 us -> none  [the longest x2 24.8 us: contract_last(): lax.dot_general(left, right, (((1,), (1,)), ((), ())), preferred_element_...]
    psum x1 -> x0, waiting for transfers between devices: 37.2 us -> none  [shards(): lax.psum(local_in, 'dp').astype(jnp.float32)]
    psum x3 -> x0, blocking collectives: 36.4 us -> none  [the longest x1 15.2 us: shards(): grad_gain = lax.psum(jnp.sum(normed_grad * centred, axis=0), ('dp', 'col'))]
    convert_element_type x5 -> x2, other arithmetic: 35.6 us -> 26 us  [shards(): return (branch, grad_patches, gwi.astype(F32), gwo.astype(F32), ggain[0])]
  transfers between devices with their start and end apart: 9 -> 0, of which waited for: 9 -> 0; matrix products, arithmetic and copies ran while one was open for 19% -> 0% of each run, Pallas kernels for 0% -> 0%
where the time goes in v1:
time: 371 us
  Pallas kernels  340 us (92%)
  other arithmetic  26 us (7%)
  local copies, waits for them, and re-layouts  4.35 us (1%)
    pallas_call x1, Pallas kernels, shards(): pl.pallas_call(functools.partial(kernel, n), out_shape=(out((tb, dl), BF1...  340 us
    convert_element_type x2, other arithmetic, shards(): return (branch, grad_patches, gwi.astype(F32), gwo.astype(F32), ggain[0])  26 us

profile of v1, /device:TPU:0, one launch (start us, length us, event | category | flops | bytes accessed | tf_op | source)
XLA Modules:
  0.0 370.6 jit_solution(9570543299559815224)
XLA Ops:
  0.6 1.3 reshape.13.gain
  1.9 339.6 %shard_map.92 = (bf16[192,1536]{1,0:T(8,128)(2,1)}, bf16[192,1536]{1,0:T(8,128)(2,1)}, bf16[1536,3072]{1,0:T(8,128)(2,1)}, bf16[3072,1536]{1,0:T(8,128)(2,1)}, f32[8,1536]{1,0:T(8,128)}) custom-call(bf16[192,1536]{1,0:T(8,128)(2,1)} %patches.1, f32[1,1536]{1,0:T(1,128)} %reshape.13.gain, bf16[1536,3072]{1,0:T(8,128)(2,1)} %w_in.1, bf16[3072,1536]{1,0:T(8,128)(2,1)} %w_out.1, ...), custom_call_target="tpu_custom_call" | custom-call | flops 43486543872 | bytes 37748736 | tf_op jit(solution)/shard_map/pallas_call | solution.py:390
  341.5 1.4 slice_reduce_fusion
  342.9 12.7 %convert_element_type.6 = f32[1536,3072]{1,0:T(8,128)} convert(bf16[1536,3072]{1,0:T(8,128)(2,1)} %get-tuple-element.12) | non-fusion elementwise | flops 4718592 | bytes 28311552 | tf_op jit(solution)/shard_map/convert_element_type | solution.py:431
  355.6 0.0 copy-start.1
  355.6 0.0 copy-start
  355.6 13.3 %convert_element_type.7 = f32[3072,1536]{1,0:T(8,128)} convert(bf16[3072,1536]{1,0:T(8,128)(2,1)} %get-tuple-element.13) | non-fusion elementwise | flops 4718592 | bytes 28311552 | tf_op jit(solution)/shard_map/convert_element_type | solution.py:431
  369.0 0.0 copy-done.1
  369.0 0.8 copy.12
  369.8 0.0 copy-done
  369.8 0.8 copy.13
Async XLA Ops:
  355.6 13.3 %copy-start.1 = (bf16[192,1536]{1,0:T(8,128)(2,1)S(1)}, bf16[192,1536]{1,0:T(8,128)(2,1)}, u32[]{:S(2)}) copy-start(bf16[192,1536]{1,0:T(8,128)(2,1)} %get-tuple-element.20) | copy-start | bytes 1769476
  355.6 14.1 %copy-start = (bf16[192,1536]{1,0:T(8,128)(2,1)S(1)}, bf16[192,1536]{1,0:T(8,128)(2,1)}, u32[]{:S(2)}) copy-start(bf16[192,1536]{1,0:T(8,128)(2,1)} %get-tuple-element.21) | copy-start | bytes 1769476

commit v2 on v1

--- a/solution.py
+++ b/solution.py
@@ -37,10 +37,338 @@
     return x * half, half + 0.5 * x * (1.0 - t * t) * (a * (1.0 + 3.0 * b * square))
 
 
+def weight_grads(tile, wd, dl, d, lhs, dstage, drecv, dsend, drsem, osem, credit):
+    def cols(t, width, start=0):
+        return pl.ds(pl.multiple_of(start + t * width, width), width)
+
+    def tile_copy(slot):
+        return pltpu.make_async_remote_copy(
+            src_ref=dstage.at[slot], dst_ref=drecv.at[slot], send_sem=dsend.at[slot], recv_sem=drsem.at[slot],
+            device_id={"dp": 1 - d}, device_id_type=MESH,
+        )
+
+    def weight_grad(left, right, out, per_row, first, last):
+        count = (out.shape[0] // tile) * per_row
+
+        def place(t):
+            if per_row == 1:
+                return out.at[cols(t, tile), :]
+            return out.at[cols(lax.div(t, jnp.int32(per_row)), tile), cols(lax.rem(t, jnp.int32(per_row)), dl)]
+
+        def result_copy(t):
+            slot = lax.rem(t, jnp.int32(2))
+            return pltpu.make_async_copy(drecv.at[slot], place(t), osem.at[slot])
+
+        def finish(t):
+            slot = lax.rem(t, jnp.int32(2))
+            tile_copy(slot).wait_send()
+            tile_copy(slot).wait_recv()
+            drecv[slot] = (dstage[slot].astype(F32) + drecv[slot].astype(F32)).astype(BF16)
+            result_copy(t).start()
+
+        def retire(t):
+            result_copy(t).wait()
+
+            def free():
+                pl.semaphore_signal(credit, inc=1, device_id={"dp": 1 - d}, device_id_type=MESH)
+
+            if last:
+                pl.when(t < count - 2)(free)
+            else:
+                free()
+
+        def step(t, carry):
+            slot = lax.rem(t, jnp.int32(2))
+            lhs[...] = left[:, cols(lax.div(t, jnp.int32(per_row)), tile)].T
+            shift = lax.rem(t, jnp.int32(per_row)) * dl
+
+            def part(p, inner):
+                dstage[slot, :, cols(p, wd)] = dot(
+                    lhs[...], right[:, pl.ds(pl.multiple_of(shift + p * wd, wd), wd)]
+                ).astype(BF16)
+                return inner
+
+            lax.fori_loop(0, dl // wd, part, 0)
+
+            @pl.when(t >= 2)
+            def _():
+                retire(t - 2)
+
+            def claim():
+                pl.semaphore_wait(credit, 1)
+
+            if first:
+                pl.when(t >= 2)(claim)
+            else:
+                claim()
+            tile_copy(slot).start()
+
+            @pl.when(t >= 1)
+            def _():
+                finish(t - 1)
+
+            return carry
+
+        lax.fori_loop(0, count, step, 0)
+        finish(jnp.int32(count - 1))
+        retire(jnp.int32(count - 2))
+        retire(jnp.int32(count - 1))
+
+    return weight_grad
+
+
+def kernel_split(
+    n, patches, gain, w_in, w_out, out_grad,
+    branch, grad_patches, gwi, gwo, ggain,
+    wi, wo, cot, nrm, hid, pg, rhg, rpre, stage, stage2, rbr, rng, st1, st2, ggr, ggd, lhs, dstage, drecv,
+    wsem, send, recv, dsend, drsem, osem, ggsem, credit,
+):
+    tb, dl = patches.shape
+    fl = w_in.shape[1]
+    sb = tb // n
+    wf = 256 if fl % 256 == 0 else 128
+    wd = 256 if dl % 256 == 0 else 128
+    tile = dstage.shape[1]
+    r, c, d = lax.axis_index("row"), lax.axis_index("col"), lax.axis_index("dp")
+    weight_grad = weight_grads(tile, wd, dl, d, lhs, dstage, drecv, dsend, drsem, osem, credit)
+
+    def rows(j):
+        return pl.ds(pl.multiple_of(j * tb, tb), tb)
+
+    def piece(j, q):
+        return pl.ds(pl.multiple_of(j * tb + q * sb, sb), sb)
+
+    def part(q):
+        return pl.ds(pl.multiple_of(q * sb, sb), sb)
+
+    def cols(t, width, start=0):
+        return pl.ds(pl.multiple_of(start + t * width, width), width)
+
+    load_out = pltpu.make_async_copy(w_out, wo, wsem.at[0])
+    load_in = pltpu.make_async_copy(w_in, wi, wsem.at[1])
+    load_out.start()
+    load_in.start()
+
+    barrier = pltpu.get_barrier_semaphore()
+    for k in range(1, n):
+        pl.semaphore_signal(barrier, inc=1, device_id={"row": flip(r, k, n)}, device_id_type=MESH)
+        pl.semaphore_signal(barrier, inc=1, device_id={"col": flip(c, k, n)}, device_id_type=MESH)
+    pl.semaphore_signal(barrier, inc=1, device_id={"dp": 1 - d}, device_id_type=MESH)
+    pl.semaphore_wait(barrier, 2 * (n - 1) + 1)
+
+    def copy(kind, src, dst, at, axis, peer):
+        return pltpu.make_async_remote_copy(
+            src_ref=src, dst_ref=dst, send_sem=send.at[kind, at], recv_sem=recv.at[kind, at],
+            device_id={axis: peer}, device_id_type=MESH,
+        )
+
+    def cot_copy(k):
+        return copy(COT, out_grad, cot.at[rows(c)], k, "col", flip(c, k, n))
+
+    def nrm_copy(k):
+        return copy(NRM, nrm.at[rows(c)], nrm.at[rows(c)], k, "col", flip(c, k, n))
+
+    def st1_copy(m):
+        return copy(ST1, st1.at[0], st1.at[m], m, "row", flip(r, m, n))
+
+    def st2_copy(m):
+        return copy(ST2, st2.at[0], st2.at[m], m, "row", flip(r, m, n))
+
+    def gg_copy(k):
+        return copy(GG, ggr.at[0], ggr.at[k], k, "col", flip(c, k, n))
+
+    def scatter_copy(kind, src, dst, j, m):
+        peer = flip(r, m, n)
+        return copy(kind, src.at[j, part(peer)], dst.at[m - 1, part(j)], j * n + m, "row", peer)
+
+    def gather_copy(kind, panel, j, m):
+        return copy(kind, panel.at[piece(j, r)], panel.at[piece(j, r)], j * n + m, "row", flip(r, m, n))
+
+    def back_copy(kind, dst, k, start):
+        j = flip(c, k, n)
+        return copy(kind, stage.at[j, :, pl.ds(start, dl)], dst.at[k - 1], k, "col", j)
+
+    cot_copy(1).start()
+    if n > 2:
+        cot_copy(2).start()
+    own_cot = pltpu.make_async_copy(out_grad, cot.at[rows(c)], wsem.at[2])
+    own_cot.start()
+
+    values = patches[...].astype(F32)
+    lane = lax.broadcasted_iota(jnp.int32, (tb, 128), 1)
+    st1[0] = jnp.where(
+        lane == 0, jnp.sum(values, axis=1, keepdims=True), jnp.sum(values * values, axis=1, keepdims=True)
+    )
+    for m in range(1, n):
+        st1_copy(m).start()
+
+    def hid_grad_terms(j):
+        def body(t, carry):
+            stage[j, :, cols(t, wf)] = dot(cot[rows(j), :], wo[cols(t, wf), :], 1, 1).astype(BF16)
+            return carry
+
+        lax.fori_loop(0, fl // wf, body, 0)
+        for m in range(1, n):
+            scatter_copy(HG, stage, rhg, j, m).start()
+
+    def pre_terms(j):
+        def body(t, carry):
+            stage2[j, :, cols(t, wf)] = dot(nrm[rows(j), :], wi[:, cols(t, wf)]).astype(BF16)
+            return carry
+
+        lax.fori_loop(0, fl // wf, body, 0)
+        for m in range(1, n):
+            scatter_copy(PRE, stage2, rpre, j, m).start()
+
+    def hidden(j):
+        for m in range(1, n):
+            scatter_copy(HG, stage, rhg, j, m).wait_recv()
+            scatter_copy(PRE, stage2, rpre, j, m).wait_recv()
+
+        def body(t, carry):
+            at = cols(t, wf)
+            pre, grad = stage2[j, part(r), at].astype(F32), stage[j, part(r), at].astype(F32)
+            for m in range(1, n):
+                pre = pre + rpre[m - 1, part(j), at].astype(F32)
+                grad = grad + rhg[m - 1, part(j), at].astype(F32)
+            activation, slope = gelu_and_slope(pre)
+            hid[piece(j, r), at] = activation.astype(BF16)
+            pg[piece(j, r), at] = (grad * slope).astype(BF16)
+            return carry
+
+        lax.fori_loop(0, fl // wf, body, 0)
+        for m in range(1, n):
+            gather_copy(HID, hid, j, m).start()
+        for m in range(1, n):
+            gather_copy(PG, pg, j, m).start()
+
+    def back(k):
+        j = flip(c, k, n)
+        for m in range(1, n):
+            scatter_copy(HG, stage, rhg, j, m).wait_send()
+        for m in range(1, n):
+            gather_copy(HID, hid, j, m).wait_recv()
+
+        def branch_body(t, carry):
+            stage[j, :, cols(t, wd)] = dot(hid[rows(j), :], wo[:, cols(t, wd)]).astype(BF16)
+            return carry
+
+        lax.fori_loop(0, dl // wd, branch_body, 0)
+        if k > 0:
+            back_copy(BR, rbr, k, 0).start()
+        for m in range(1, n):
+            gather_copy(PG, pg, j, m).wait_recv()
+
+        def grad_body(t, carry):
+            stage[j, :, cols(t, wd, dl)] = dot(pg[rows(j), :], wi[cols(t, wd), :], 1, 1).astype(BF16)
+            return carry
+
+        lax.fori_loop(0, dl // wd, grad_body, 0)
+        if k > 0:
+            back_copy(NG, rng, k, dl).start()
+
+    own_cot.wait()
+    load_out.wait()
+    hid_grad_terms(c)
+
+    sums = st1[0]
+    for m in range(1, n):
+        st1_copy(m).wait_recv()
+        sums = sums + st1[m]
+    average = sums[:, 0:1] / D
+    inverse = lax.rsqrt(sums[:, 1:2] / D - average * average + 1e-06)
+    nrm[rows(c), :] = ((patches[...].astype(F32) - average) * inverse * gain[...]).astype(BF16)
+    nrm_copy(1).start()
+    if n > 2:
+        nrm_copy(2).start()
+    load_in.wait()
+    pre_terms(c)
+
+    for k in range(1, n):
+        cot_copy(k).wait_recv()
+        if k + 2 < n:
+            cot_copy(k).wait_send()
+            cot_copy(k + 2).start()
+        hid_grad_terms(flip(c, k, n))
+        nrm_copy(k).wait_recv()
+        if k + 2 < n:
+            nrm_copy(k).wait_send()
+            nrm_copy(k + 2).start()
+        pre_terms(flip(c, k, n))
+        hidden(flip(c, k - 1, n))
+        if k > 1:
+            back(k - 2)
+    hidden(flip(c, n - 1, n))
+    for k in range(max(n - 2, 0), n):
+        back(k)
+
+    weight_grad(hid, cot, gwo, 1, True, False)
+
+    def sum_back(dst, start):
+        total = stage[c, :, pl.ds(start, dl)].astype(F32)
+        for k in range(1, n):
+            total = total + dst[k - 1].astype(F32)
+        return total
+
+    for k in range(1, n):
+        back_copy(NG, rng, k, dl).wait_recv()
+    total = sum_back(rng, dl)
+    weighted = total * ((patches[...].astype(F32) - average) * inverse)
+    ggr[0] = jnp.broadcast_to(jnp.sum(weighted, axis=0, keepdims=True), (8, dl))
+    st2[0] = jnp.where(
+        lane == 0, jnp.sum(total * gain[...], axis=1, keepdims=True),
+        jnp.sum(weighted * gain[...], axis=1, keepdims=True),
+    )
+    for m in range(1, n):
+        st2_copy(m).start()
+    for k in range(1, n):
+        gg_copy(k).start()
+    for k in range(1, n):
+        back_copy(BR, rbr, k, 0).wait_recv()
+    branch[...] = sum_back(rbr, 0).astype(BF16)
+    own = ggr[0]
+    for k in range(1, n):
+        gg_copy(k).wait_recv()
+        own = own + ggr[k]
+    ggd[0] = own
+    gain_copy = pltpu.make_async_remote_copy(
+        src_ref=ggd.at[0], dst_ref=ggd.at[1], send_sem=ggsem.at[0], recv_sem=ggsem.at[1],
+        device_id={"dp": 1 - d}, device_id_type=MESH,
+    )
+    gain_copy.start()
+
+    weight_grad(nrm, pg, gwi, fl // dl, False, True)
+
+    sums = st2[0]
+    for m in range(1, n):
+        st2_copy(m).wait_recv()
+        sums = sums + st2[m]
+    first, second = sums[:, 0:1] / D, sums[:, 1:2] / D
+    centred = (patches[...].astype(F32) - average) * inverse
+    grad_patches[...] = (inverse * (sum_back(rng, dl) * gain[...] - first - centred * second)).astype(BF16)
+    gain_copy.wait()
+    ggain[...] = ggd[0] + ggd[1]
+
+    for m in range(1, n):
+        st1_copy(m).wait_send()
+        st2_copy(m).wait_send()
+        gg_copy(m).wait_send()
+        back_copy(BR, rbr, m, 0).wait_send()
+        back_copy(NG, rng, m, dl).wait_send()
+        if m + 2 >= n:
+            cot_copy(m).wait_send()
+            nrm_copy(m).wait_send()
+        for k in range(n):
+            j = flip(c, k, n)
+            scatter_copy(PRE, stage2, rpre, j, m).wait_send()
+            gather_copy(HID, hid, j, m).wait_send()
+            gather_copy(PG, pg, j, m).wait_send()
+
+
 def kernel(
     n, patches, gain, w_in, w_out, out_grad,
     branch, grad_patches, gwi, gwo, ggain,
-    wi, wo, cot, nrm, hid, pg, rhg, rpre, stage, rbr, rng, st1, st2, ggr, ggd, lhs, dstage, drecv, obuf,
+    wi, wo, cot, nrm, hid, pg, rhg, rpre, stage, rbr, rng, st1, st2, ggr, ggd, lhs, dstage, drecv,
     wsem, send, recv, dsend, drsem, osem, ggsem, credit,
 ):
     tb, dl = patches.shape
@@ -91,7 +419,8 @@
 
     for k in range(1, n):
         cot_copy(k).start()
-    cot[rows(c), :] = out_grad[...]
+    own_cot = pltpu.make_async_copy(out_grad, cot.at[rows(c)], wsem.at[2])
+    own_cot.start()
 
     values = patches[...].astype(F32)
     lane = lax.broadcasted_iota(jnp.int32, (tb, 128), 1)
@@ -138,6 +467,7 @@
     def pre_product(left, t):
         return dot(left, wi[:, cols(t, wf)])
 
+    own_cot.wait()
     load_out.wait()
     scatter_row(HG, jnp.int32(0), cot, hg_product, rhg)
 
@@ -236,77 +566,7 @@
 
     lax.fori_loop(0, n, branch_step, 0)
 
-    def tile_copy(slot):
-        return pltpu.make_async_remote_copy(
-            src_ref=dstage.at[slot], dst_ref=drecv.at[slot], send_sem=dsend.at[slot], recv_sem=drsem.at[slot],
-            device_id={"dp": 1 - d}, device_id_type=MESH,
-        )
-
-    def weight_grad(left, right, out, per_row, first, last):
-        count = (out.shape[0] // tile) * per_row
-
-        def place(t):
-            if per_row == 1:
-                return out.at[cols(t, tile), :]
-            return out.at[cols(lax.div(t, jnp.int32(per_row)), tile), cols(lax.rem(t, jnp.int32(per_row)), dl)]
-
-        def result_copy(t):
-            slot = lax.rem(t, jnp.int32(2))
-            return pltpu.make_async_copy(obuf.at[slot], place(t), osem.at[slot])
-
-        def finish(t):
-            slot = lax.rem(t, jnp.int32(2))
-            tile_copy(slot).wait_send()
-            tile_copy(slot).wait_recv()
-
-            @pl.when(t >= 2)
-            def _():
-                result_copy(t - 2).wait()
-
-            obuf[slot] = (dstage[slot].astype(F32) + drecv[slot].astype(F32)).astype(BF16)
-            result_copy(t).start()
-
-            def free():
-                pl.semaphore_signal(credit, inc=1, device_id={"dp": 1 - d}, device_id_type=MESH)
-
-            if last:
-                pl.when(t < count - 2)(free)
-            else:
-                free()
-
-        def step(t, carry):
-            slot = lax.rem(t, jnp.int32(2))
-            lhs[...] = left[:, cols(lax.div(t, jnp.int32(per_row)), tile)].T
-            shift = lax.rem(t, jnp.int32(per_row)) * dl
-
-            def part(p, inner):
-                dstage[slot, :, cols(p, wd)] = dot(
-                    lhs[...], right[:, pl.ds(pl.multiple_of(shift + p * wd, wd), wd)]
-                ).astype(BF16)
-                return inner
-
-            lax.fori_loop(0, dl // wd, part, 0)
-
-            def claim():
-                pl.semaphore_wait(credit, 1)
-
-            if first:
-                pl.when(t >= 2)(claim)
-            else:
-                claim()
-            tile_copy(slot).start()
-
-            @pl.when(t >= 1)
-            def _():
-                finish(t - 1)
-
-            return carry
-
-        lax.fori_loop(0, count, step, 0)
-        finish(jnp.int32(count - 1))
-        result_copy(jnp.int32(count - 2)).wait()
-        result_copy(jnp.int32(count - 1)).wait()
-
+    weight_grad = weight_grads(tile, wd, dl, d, lhs, dstage, drecv, dsend, drsem, osem, credit)
     weight_grad(hid, cot, gwo, 1, True, False)
 
     def ng_step(k, carry):
@@ -387,12 +647,20 @@
     hbm = pl.BlockSpec(memory_space=pl.ANY)
     out = jax.ShapeDtypeStruct
     flops = 12 * n * tb * dl * fl
+    split = tb % (16 * n) == 0
+    block = pltpu.VMEM((n, tb, fl), BF16)
+    if split:
+        body = kernel_split
+        landing = [pltpu.VMEM((n - 1, tb, fl), BF16)] * 2 + [block] * 2 + [pltpu.VMEM((n - 1, tb, dl), BF16)] * 2
+    else:
+        body = kernel
+        landing = [block] * 3 + [pltpu.VMEM((n, tb, dl), BF16)] * 2
     branch, grad_patches, gwi, gwo, ggain = pl.pallas_call(
-        functools.partial(kernel, n),
+        functools.partial(body, n),
         out_shape=(
             out((tb, dl), BF16), out((tb, dl), BF16), out((dl, fl), BF16), out((fl, dl), BF16), out((8, dl), F32),
         ),
-        in_specs=[vmem, vmem, hbm, hbm, vmem],
+        in_specs=[vmem, vmem, hbm, hbm, hbm],
         out_specs=(vmem, vmem, hbm, hbm, vmem),
         scratch_shapes=[
             pltpu.VMEM((dl, fl), BF16),
@@ -401,11 +669,7 @@
             pltpu.VMEM((n * tb, dl), BF16),
             pltpu.VMEM((n * tb, fl), BF16),
             pltpu.VMEM((n * tb, fl), BF16),
-            pltpu.VMEM((n, tb, fl), BF16),
-            pltpu.VMEM((n, tb, fl), BF16),
-            pltpu.VMEM((n, tb, fl), BF16),
-            pltpu.VMEM((n, tb, dl), BF16),
-            pltpu.VMEM((n, tb, dl), BF16),
+            *landing,
             pltpu.VMEM((n, tb, 128), F32),
             pltpu.VMEM((n, tb, 128), F32),
             pltpu.VMEM((n, 8, dl), F32),
@@ -413,10 +677,9 @@
             pltpu.VMEM((tile, n * tb), BF16),
             pltpu.VMEM((2, tile, dl), BF16),
             pltpu.VMEM((2, tile, dl), BF16),
-            pltpu.VMEM((2, tile, dl), BF16),
-            pltpu.SemaphoreType.DMA((2,)),
-            pltpu.SemaphoreType.DMA((11, n)),
-            pltpu.SemaphoreType.DMA((11, n)),
+            pltpu.SemaphoreType.DMA((3,)),
+            pltpu.SemaphoreType.DMA((11, n * n if split else n)),
+            pltpu.SemaphoreType.DMA((11, n * n if split else n)),
             pltpu.SemaphoreType.DMA((2,)),
             pltpu.SemaphoreType.DMA((2,)),
             pltpu.SemaphoreType.DMA((2,)),

time: 371 us -> 369 us (level)
  no operation moved by 1% of the time
where the time goes in v2:
time: 369 us
  Pallas kernels  338 us (92%)
  other arithmetic  26 us (7%)
  local copies, waits for them, and re-layouts  4.35 us (1%)
    pallas_call x1, Pallas kernels, shards(): pl.pallas_call(functools.partial(body, n), out_shape=(out((tb, dl), BF16)...  338 us
    convert_element_type x2, other arithmetic, shards(): return (branch, grad_patches, gwi.astype(F32), gwo.astype(F32), ggain[0])  26 us

profile of v2, /device:TPU:0, one launch (start us, length us, event | category | flops | bytes accessed | tf_op | source)
XLA Modules:
  0.0 369.2 jit_solution(10090013712939302464)
XLA Ops:
  0.6 1.3 reshape.13.gain
  1.9 338.1 %shard_map.92 = (bf16[192,1536]{1,0:T(8,128)(2,1)}, bf16[192,1536]{1,0:T(8,128)(2,1)}, bf16[1536,3072]{1,0:T(8,128)(2,1)}, bf16[3072,1536]{1,0:T(8,128)(2,1)}, f32[8,1536]{1,0:T(8,128)}) custom-call(bf16[192,1536]{1,0:T(8,128)(2,1)} %patches.1, f32[1,1536]{1,0:T(1,128)} %reshape.13.gain, bf16[1536,3072]{1,0:T(8,128)(2,1)} %w_in.1, bf16[3072,1536]{1,0:T(8,128)(2,1)} %w_out.1, ...), custom_call_target="tpu_custom_call" | custom-call | flops 43486543872 | bytes 37748736 | tf_op jit(solution)/shard_map/pallas_call | solution.py:658
  340.1 1.4 slice_reduce_fusion
  341.5 12.7 %convert_element_type.6 = f32[1536,3072]{1,0:T(8,128)} convert(bf16[1536,3072]{1,0:T(8,128)(2,1)} %get-tuple-element.12) | non-fusion elementwise | flops 4718592 | bytes 28311552 | tf_op jit(solution)/shard_map/convert_element_type | solution.py:694
  354.2 0.0 copy-start.1
  354.2 0.0 copy-start
  354.2 13.3 %convert_element_type.7 = f32[3072,1536]{1,0:T(8,128)} convert(bf16[3072,1536]{1,0:T(8,128)(2,1)} %get-tuple-element.13) | non-fusion elementwise | flops 4718592 | bytes 28311552 | tf_op jit(solution)/shard_map/convert_element_type | solution.py:694
  367.5 0.0 copy-done.1
  367.5 0.8 copy.12
  368.3 0.0 copy-done
  368.4 0.8 copy.13
Async XLA Ops:
  354.2 13.3 %copy-start.1 = (bf16[192,1536]{1,0:T(8,128)(2,1)S(1)}, bf16[192,1536]{1,0:T(8,128)(2,1)}, u32[]{:S(2)}) copy-start(bf16[192,1536]{1,0:T(8,128)(2,1)} %get-tuple-element.20) | copy-start | bytes 1769476
  354.2 14.1 %copy-start = (bf16[192,1536]{1,0:T(8,128)(2,1)S(1)}, bf16[192,1536]{1,0:T(8,128)(2,1)}, u32[]{:S(2)}) copy-start(bf16[192,1536]{1,0:T(8,128)(2,1)} %get-tuple-element.21) | copy-start | bytes 1769476

commit v3 on v2

--- a/solution.py
+++ b/solution.py
@@ -37,33 +37,36 @@
     return x * half, half + 0.5 * x * (1.0 - t * t) * (a * (1.0 + 3.0 * b * square))
 
 
-def weight_grads(tile, wd, dl, d, lhs, dstage, drecv, dsend, drsem, osem, credit):
+def weight_grads(d, lhs, tm, tn, outgoing, incoming, dsend, drsem, osem, credit):
     def cols(t, width, start=0):
         return pl.ds(pl.multiple_of(start + t * width, width), width)
 
     def tile_copy(slot):
         return pltpu.make_async_remote_copy(
-            src_ref=dstage.at[slot], dst_ref=drecv.at[slot], send_sem=dsend.at[slot], recv_sem=drsem.at[slot],
+            src_ref=outgoing(slot), dst_ref=incoming(slot), send_sem=dsend.at[slot], recv_sem=drsem.at[slot],
             device_id={"dp": 1 - d}, device_id_type=MESH,
         )
 
-    def weight_grad(left, right, out, per_row, first, last):
-        count = (out.shape[0] // tile) * per_row
+    def weight_grad(left, right, out, first, last):
+        per_row = out.shape[1] // tn
+        count = (out.shape[0] // tm) * per_row
+
+        def across(t):
+            return cols(lax.rem(t, jnp.int32(per_row)), tn)
 
         def place(t):
-            if per_row == 1:
-                return out.at[cols(t, tile), :]
-            return out.at[cols(lax.div(t, jnp.int32(per_row)), tile), cols(lax.rem(t, jnp.int32(per_row)), dl)]
+            return out.at[cols(lax.div(t, jnp.int32(per_row)), tm), across(t)]
 
         def result_copy(t):
             slot = lax.rem(t, jnp.int32(2))
-            return pltpu.make_async_copy(drecv.at[slot], place(t), osem.at[slot])
+            return pltpu.make_async_copy(incoming(slot), place(t), osem.at[slot])
 
         def finish(t):
             slot = lax.rem(t, jnp.int32(2))
             tile_copy(slot).wait_send()
             tile_copy(slot).wait_recv()
-            drecv[slot] = (dstage[slot].astype(F32) + drecv[slot].astype(F32)).astype(BF16)
+            total = outgoing(slot)[...].astype(F32) + incoming(slot)[...].astype(F32)
+            incoming(slot)[...] = total.astype(BF16)
             result_copy(t).start()
 
         def retire(t):
@@ -79,16 +82,12 @@
 
         def step(t, carry):
             slot = lax.rem(t, jnp.int32(2))
-            lhs[...] = left[:, cols(lax.div(t, jnp.int32(per_row)), tile)].T
-            shift = lax.rem(t, jnp.int32(per_row)) * dl
-
-            def part(p, inner):
-                dstage[slot, :, cols(p, wd)] = dot(
-                    lhs[...], right[:, pl.ds(pl.multiple_of(shift + p * wd, wd), wd)]
-                ).astype(BF16)
-                return inner
-
-            lax.fori_loop(0, dl // wd, part, 0)
+
+            @pl.when(lax.rem(t, jnp.int32(per_row)) == 0)
+            def _():
+                lhs[...] = left[:, cols(lax.div(t, jnp.int32(per_row)), tm)].T
+
+            outgoing(slot)[...] = dot(lhs[...], right[:, across(t)]).astype(BF16)
 
             @pl.when(t >= 2)
             def _():
@@ -120,18 +119,15 @@
 def kernel_split(
     n, patches, gain, w_in, w_out, out_grad,
     branch, grad_patches, gwi, gwo, ggain,
-    wi, wo, cot, nrm, hid, pg, rhg, rpre, stage, stage2, rbr, rng, st1, st2, ggr, ggd, lhs, dstage, drecv,
+    wi, wo, cot, nrm, hid, pg, rhg, rpre, stage, stage2, rbr, rng, st1, st2, ggr, ggd, lhs,
     wsem, send, recv, dsend, drsem, osem, ggsem, credit,
 ):
     tb, dl = patches.shape
     fl = w_in.shape[1]
     sb = tb // n
-    wf = 256 if fl % 256 == 0 else 128
-    wd = 256 if dl % 256 == 0 else 128
-    tile = dstage.shape[1]
+    wf = wd = dl // 2
+    wg = 256
     r, c, d = lax.axis_index("row"), lax.axis_index("col"), lax.axis_index("dp")
-    weight_grad = weight_grads(tile, wd, dl, d, lhs, dstage, drecv, dsend, drsem, osem, credit)
-
     def rows(j):
         return pl.ds(pl.multiple_of(j * tb, tb), tb)
 
@@ -143,6 +139,13 @@
 
     def cols(t, width, start=0):
         return pl.ds(pl.multiple_of(start + t * width, width), width)
+
+    tm, tn = lhs.shape[0], fl // 4
+
+    weight_grad = weight_grads(
+        d, lhs, tm, tn, lambda slot: stage2.at[pl.ds(0, tm), cols(slot, tn)],
+        lambda slot: stage2.at[pl.ds(0, tm), cols(slot + 2, tn)], dsend, drsem, osem, credit,
+    )
 
     load_out = pltpu.make_async_copy(w_out, wo, wsem.at[0])
     load_in = pltpu.make_async_copy(w_in, wi, wsem.at[1])
@@ -179,7 +182,8 @@
 
     def scatter_copy(kind, src, dst, j, m):
         peer = flip(r, m, n)
-        return copy(kind, src.at[j, part(peer)], dst.at[m - 1, part(j)], j * n + m, "row", peer)
+        mine = src.at[piece(j, peer)] if kind == PRE else src.at[j, part(peer)]
+        return copy(kind, mine, dst.at[m - 1, part(j)], j * n + m, "row", peer)
 
     def gather_copy(kind, panel, j, m):
         return copy(kind, panel.at[piece(j, r)], panel.at[piece(j, r)], j * n + m, "row", flip(r, m, n))
@@ -202,23 +206,33 @@
     for m in range(1, n):
         st1_copy(m).start()
 
-    def hid_grad_terms(j):
+    def pair(p):
+        return pl.ds(pl.multiple_of(p * 2 * tb, 2 * tb), 2 * tb)
+
+    def store(ref, p, at, term):
+        term = term.astype(BF16)
+        ref[2 * p, :, at] = term[:tb]
+        ref[2 * p + 1, :, at] = term[tb:]
+
+    def hid_grad_terms(p):
         def body(t, carry):
-            stage[j, :, cols(t, wf)] = dot(cot[rows(j), :], wo[cols(t, wf), :], 1, 1).astype(BF16)
+            store(stage, p, cols(t, wf), dot(cot[pair(p), :], wo[cols(t, wf), :], 1, 1))
             return carry
 
         lax.fori_loop(0, fl // wf, body, 0)
-        for m in range(1, n):
-            scatter_copy(HG, stage, rhg, j, m).start()
-
-    def pre_terms(j):
+        for j in (2 * p, 2 * p + 1):
+            for m in range(1, n):
+                scatter_copy(HG, stage, rhg, j, m).start()
+
+    def pre_terms(p):
         def body(t, carry):
-            stage2[j, :, cols(t, wf)] = dot(nrm[rows(j), :], wi[:, cols(t, wf)]).astype(BF16)
+            stage2[pair(p), cols(t, wf)] = dot(nrm[pair(p), :], wi[:, cols(t, wf)]).astype(BF16)
             return carry
 
         lax.fori_loop(0, fl // wf, body, 0)
-        for m in range(1, n):
-            scatter_copy(PRE, stage2, rpre, j, m).start()
+        for j in (2 * p, 2 * p + 1):
+            for m in range(1, n):
+                scatter_copy(PRE, stage2, rpre, j, m).start()
 
     def hidden(j):
         for m in range(1, n):
@@ -226,8 +240,8 @@
             scatter_copy(PRE, stage2, rpre, j, m).wait_recv()
 
         def body(t, carry):
-            at = cols(t, wf)
-            pre, grad = stage2[j, part(r), at].astype(F32), stage[j, part(r), at].astype(F32)
+            at = cols(t, wg)
+            pre, grad = stage2[piece(j, r), at].astype(F32), stage[j, part(r), at].astype(F32)
             for m in range(1, n):
                 pre = pre + rpre[m - 1, part(j), at].astype(F32)
                 grad = grad + rhg[m - 1, part(j), at].astype(F32)
@@ -236,40 +250,43 @@
             pg[piece(j, r), at] = (grad * slope).astype(BF16)
             return carry
 
-        lax.fori_loop(0, fl // wf, body, 0)
+        lax.fori_loop(0, fl // wg, body, 0)
         for m in range(1, n):
             gather_copy(HID, hid, j, m).start()
         for m in range(1, n):
             gather_copy(PG, pg, j, m).start()
 
-    def back(k):
-        j = flip(c, k, n)
-        for m in range(1, n):
-            scatter_copy(HG, stage, rhg, j, m).wait_send()
-        for m in range(1, n):
-            gather_copy(HID, hid, j, m).wait_recv()
-
-        def branch_body(t, carry):
-            stage[j, :, cols(t, wd)] = dot(hid[rows(j), :], wo[:, cols(t, wd)]).astype(BF16)
+    def back_branch(p, ks):
+        for j in (2 * p, 2 * p + 1):
+            for m in range(1, n):
+                scatter_copy(HG, stage, rhg, j, m).wait_send()
+                gather_copy(HID, hid, j, m).wait_recv()
+
+        def body(t, carry):
+            store(stage, p, cols(t, wd), dot(hid[pair(p), :], wo[:, cols(t, wd)]))
             return carry
 
-        lax.fori_loop(0, dl // wd, branch_body, 0)
-        if k > 0:
-            back_copy(BR, rbr, k, 0).start()
-        for m in range(1, n):
-            gather_copy(PG, pg, j, m).wait_recv()
-
-        def grad_body(t, carry):
-            stage[j, :, cols(t, wd, dl)] = dot(pg[rows(j), :], wi[cols(t, wd), :], 1, 1).astype(BF16)
+        lax.fori_loop(0, dl // wd, body, 0)
+        for k in ks:
+            if k > 0:
+                back_copy(BR, rbr, k, 0).start()
+
+    def back_grad(p, ks):
+        for j in (2 * p, 2 * p + 1):
+            for m in range(1, n):
+                gather_copy(PG, pg, j, m).wait_recv()
+
+        def body(t, carry):
+            store(stage, p, cols(t, wd, dl), dot(pg[pair(p), :], wi[cols(t, wd), :], 1, 1))
             return carry
 
-        lax.fori_loop(0, dl // wd, grad_body, 0)
-        if k > 0:
-            back_copy(NG, rng, k, dl).start()
+        lax.fori_loop(0, dl // wd, body, 0)
+        for k in ks:
+            if k > 0:
+                back_copy(NG, rng, k, dl).start()
 
     own_cot.wait()
     load_out.wait()
-    hid_grad_terms(c)
 
     sums = st1[0]
     for m in range(1, n):
@@ -282,27 +299,43 @@
     if n > 2:
         nrm_copy(2).start()
     load_in.wait()
-    pre_terms(c)
-
-    for k in range(1, n):
-        cot_copy(k).wait_recv()
-        if k + 2 < n:
-            cot_copy(k).wait_send()
-            cot_copy(k + 2).start()
-        hid_grad_terms(flip(c, k, n))
-        nrm_copy(k).wait_recv()
-        if k + 2 < n:
-            nrm_copy(k).wait_send()
-            nrm_copy(k + 2).start()
-        pre_terms(flip(c, k, n))
-        hidden(flip(c, k - 1, n))
-        if k > 1:
-            back(k - 2)
-    hidden(flip(c, n - 1, n))
-    for k in range(max(n - 2, 0), n):
-        back(k)
-
-    weight_grad(hid, cot, gwo, 1, True, False)
+
+    near = lax.div(c, jnp.int32(2))
+    pairs = [flip(near, h, n // 2) for h in range(n // 2)]
+
+    def arrived(copy_of, h):
+        for k in (2 * h, 2 * h + 1):
+            if k > 0:
+                copy_of(k).wait_recv()
+                if k + 2 < n:
+                    copy_of(k).wait_send()
+                    copy_of(k + 2).start()
+
+    def members(h):
+        return 2 * h, 2 * h + 1
+
+    for h in range(n // 2):
+        arrived(cot_copy, h)
+        hid_grad_terms(pairs[h])
+        if h > 0:
+            hidden(2 * pairs[h - 1])
+            hidden(2 * pairs[h - 1] + 1)
+        arrived(nrm_copy, h)
+        pre_terms(pairs[h])
+        if h > 0:
+            back_branch(pairs[h - 1], members(h - 1))
+            back_grad(pairs[h - 1], members(h - 1))
+    last = n // 2 - 1
+    hidden(2 * pairs[last])
+    hidden(2 * pairs[last] + 1)
+    back_branch(pairs[last], members(last))
+    back_grad(pairs[last], members(last))
+
+    for m in range(1, n):
+        for k in range(n):
+            scatter_copy(PRE, stage2, rpre, flip(c, k, n), m).wait_send()
+    pl.semaphore_signal(credit, inc=2, device_id={"dp": 1 - d}, device_id_type=MESH)
+    weight_grad(hid, cot, gwo, False, False)
 
     def sum_back(dst, start):
         total = stage[c, :, pl.ds(start, dl)].astype(F32)
@@ -337,7 +370,7 @@
     )
     gain_copy.start()
 
-    weight_grad(nrm, pg, gwi, fl // dl, False, True)
+    weight_grad(nrm, pg, gwi, False, True)
 
     sums = st2[0]
     for m in range(1, n):
@@ -360,7 +393,6 @@
             nrm_copy(m).wait_send()
         for k in range(n):
             j = flip(c, k, n)
-            scatter_copy(PRE, stage2, rpre, j, m).wait_send()
             gather_copy(HID, hid, j, m).wait_send()
             gather_copy(PG, pg, j, m).wait_send()
 
@@ -375,7 +407,6 @@
     fl = w_in.shape[1]
     wf = 256 if fl % 256 == 0 else 128
     wd = 256 if dl % 256 == 0 else 128
-    tile = dstage.shape[1]
     r, c, d = lax.axis_index("row"), lax.axis_index("col"), lax.axis_index("dp")
 
     def rows(j):
@@ -566,8 +597,10 @@
 
     lax.fori_loop(0, n, branch_step, 0)
 
-    weight_grad = weight_grads(tile, wd, dl, d, lhs, dstage, drecv, dsend, drsem, osem, credit)
-    weight_grad(hid, cot, gwo, 1, True, False)
+    weight_grad = weight_grads(
+        d, lhs, *dstage.shape[1:], lambda slot: dstage.at[slot], lambda slot: drecv.at[slot], dsend, drsem, osem, credit,
+    )
+    weight_grad(hid, cot, gwo, True, False)
 
     def ng_step(k, carry):
         source = flip(r, k, n)
@@ -581,7 +614,7 @@
         return carry
 
     lax.fori_loop(0, n, ng_step, 0)
-    weight_grad(nrm, pg, gwi, fl // dl, False, True)
+    weight_grad(nrm, pg, gwi, False, True)
 
     for k in range(1, n):
         arrival(NG, rng.at[flip(c, k, n)], flip(c, k, n), "col")
@@ -642,7 +675,8 @@
 def shards(n, patches, norm_gain, w_in, w_out, out_grad):
     tb, dl = patches.shape
     fl = w_in.shape[1]
-    tile = 256 if dl % 256 == 0 and fl % 256 == 0 else 128
+    tm = 512 if dl % 512 == 0 and fl % 512 == 0 else 128
+    tn = dl // 2 if dl % 256 == 0 else dl
     vmem = pl.BlockSpec(memory_space=pltpu.VMEM)
     hbm = pl.BlockSpec(memory_space=pl.ANY)
     out = jax.ShapeDtypeStruct
@@ -651,9 +685,11 @@
     block = pltpu.VMEM((n, tb, fl), BF16)
     if split:
         body = kernel_split
-        landing = [pltpu.VMEM((n - 1, tb, fl), BF16)] * 2 + [block] * 2 + [pltpu.VMEM((n - 1, tb, dl), BF16)] * 2
+        exchange = []
+        landing = [pltpu.VMEM((n - 1, tb, fl), BF16)] * 2 + [block, pltpu.VMEM((n * tb, fl), BF16)] + [pltpu.VMEM((n - 1, tb, dl), BF16)] * 2
     else:
         body = kernel
+        exchange = [pltpu.VMEM((2, tm, tn), BF16)] * 2
         landing = [block] * 3 + [pltpu.VMEM((n, tb, dl), BF16)] * 2
     branch, grad_patches, gwi, gwo, ggain = pl.pallas_call(
         functools.partial(body, n),
@@ -674,9 +710,8 @@
             pltpu.VMEM((n, tb, 128), F32),
             pltpu.VMEM((n, 8, dl), F32),
             pltpu.VMEM((2, 8, dl), F32),
-            pltpu.VMEM((tile, n * tb), BF16),
-            pltpu.VMEM((2, tile, dl), BF16),
-            pltpu.VMEM((2, tile, dl), BF16),
+            pltpu.VMEM((tm, n * tb), BF16),
+            *exchange,
             pltpu.SemaphoreType.DMA((3,)),
             pltpu.SemaphoreType.DMA((11, n * n if split else n)),
             pltpu.SemaphoreType.DMA((11, n * n if split else n)),

time: 369 us -> 406 us (1.10)
  Pallas kernels: 338 us -> 375 us
    pallas_call x1, Pallas kernels: 338 us -> 375 us  [shards(): pl.pallas_call(functools.partial(body, n), out_shape=(out((tb, dl), BF16)...]
where the time goes in v3:
time: 406 us
  Pallas kernels  375 us (92%)
  other arithmetic  26 us (6%)
  local copies, waits for them, and re-layouts  4.35 us (1%)
    pallas_call x1, Pallas kernels, shards(): pl.pallas_call(functools.partial(body, n), out_shape=(out((tb, dl), BF16)...  375 us
    convert_element_type x2, other arithmetic, shards(): return (branch, grad_patches, gwi.astype(F32), gwo.astype(F32), ggain[0])  26 us

profile of v3, /device:TPU:0, one launch (start us, length us, event | category | flops | bytes accessed | tf_op | source)
XLA Modules:
  0.0 405.9 jit_solution(4848323217690210414)
XLA Ops:
  0.6 1.3 reshape.13.gain
  1.9 374.9 %shard_map.92 = (bf16[192,1536]{1,0:T(8,128)(2,1)}, bf16[192,1536]{1,0:T(8,128)(2,1)}, bf16[1536,3072]{1,0:T(8,128)(2,1)}, bf16[3072,1536]{1,0:T(8,128)(2,1)}, f32[8,1536]{1,0:T(8,128)}) custom-call(bf16[192,1536]{1,0:T(8,128)(2,1)} %patches.1, f32[1,1536]{1,0:T(1,128)} %reshape.13.gain, bf16[1536,3072]{1,0:T(8,128)(2,1)} %w_in.1, bf16[3072,1536]{1,0:T(8,128)(2,1)} %w_out.1, ...), custom_call_target="tpu_custom_call" | custom-call | flops 43486543872 | bytes 37748736 | tf_op jit(solution)/shard_map/pallas_call | solution.py:694
  376.8 1.4 slice_reduce_fusion
  378.2 12.7 %convert_element_type.6 = f32[1536,3072]{1,0:T(8,128)} convert(bf16[1536,3072]{1,0:T(8,128)(2,1)} %get-tuple-element.12) | non-fusion elementwise | flops 4718592 | bytes 28311552 | tf_op jit(solution)/shard_map/convert_element_type | solution.py:729
  391.0 0.0 copy-start.1
  391.0 0.0 copy-start
  391.0 13.3 %convert_element_type.7 = f32[3072,1536]{1,0:T(8,128)} convert(bf16[3072,1536]{1,0:T(8,128)(2,1)} %get-tuple-element.13) | non-fusion elementwise | flops 4718592 | bytes 28311552 | tf_op jit(solution)/shard_map/convert_element_type | solution.py:729
  404.3 0.0 copy-done.1
  404.3 0.8 copy.12
  405.1 0.0 copy-done
  405.1 0.8 copy.13
Async XLA Ops:
  391.0 13.3 %copy-start.1 = (bf16[192,1536]{1,0:T(8,128)(2,1)S(1)}, bf16[192,1536]{1,0:T(8,128)(2,1)}, u32[]{:S(2)}) copy-start(bf16[192,1536]{1,0:T(8,128)(2,1)} %get-tuple-element.20) | copy-start | bytes 1769476
  391.0 14.1 %copy-start = (bf16[192,1536]{1,0:T(8,128)(2,1)S(1)}, bf16[192,1536]{1,0:T(8,128)(2,1)}, u32[]{:S(2)}) copy-start(bf16[192,1536]{1,0:T(8,128)(2,1)} %get-tuple-element.21) | copy-start | bytes 1769476

commit v4 on v2

--- a/solution.py
+++ b/solution.py
@@ -303,6 +303,7 @@
         back(k)
 
     weight_grad(hid, cot, gwo, 1, True, False)
+    weight_grad(nrm, pg, gwi, fl // dl, False, True)
 
     def sum_back(dst, start):
         total = stage[c, :, pl.ds(start, dl)].astype(F32)
@@ -336,8 +337,6 @@
         device_id={"dp": 1 - d}, device_id_type=MESH,
     )
     gain_copy.start()
-
-    weight_grad(nrm, pg, gwi, fl // dl, False, True)
 
     sums = st2[0]
     for m in range(1, n):

time: 369 us -> 337 us (0.913)
  Pallas kernels: 338 us -> 306 us
    pallas_call x1, Pallas kernels: 338 us -> 306 us  [shards(): pl.pallas_call(functools.partial(body, n), out_shape=(out((tb, dl), BF16)...]
where the time goes in v4:
time: 337 us
  Pallas kernels  306 us (91%)
  other arithmetic  26 us (8%)
  local copies, waits for them, and re-layouts  4.35 us (1%)
    pallas_call x1, Pallas kernels, shards(): pl.pallas_call(functools.partial(body, n), out_shape=(out((tb, dl), BF16)...  306 us
    convert_element_type x2, other arithmetic, shards(): return (branch, grad_patches, gwi.astype(F32), gwo.astype(F32), ggain[0])  26 us

profile of v4, /device:TPU:0, one launch (start us, length us, event | category | flops | bytes accessed | tf_op | source)
XLA Modules:
  0.0 337.1 jit_solution(14238943018831793819)
XLA Ops:
  0.6 1.3 reshape.13.gain
  1.9 306.1 %shard_map.92 = (bf16[192,1536]{1,0:T(8,128)(2,1)}, bf16[192,1536]{1,0:T(8,128)(2,1)}, bf16[1536,3072]{1,0:T(8,128)(2,1)}, bf16[3072,1536]{1,0:T(8,128)(2,1)}, f32[8,1536]{1,0:T(8,128)}) custom-call(bf16[192,1536]{1,0:T(8,128)(2,1)} %patches.1, f32[1,1536]{1,0:T(1,128)} %reshape.13.gain, bf16[1536,3072]{1,0:T(8,128)(2,1)} %w_in.1, bf16[3072,1536]{1,0:T(8,128)(2,1)} %w_out.1, ...), custom_call_target="tpu_custom_call" | custom-call | flops 43486543872 | bytes 37748736 | tf_op jit(solution)/shard_map/pallas_call | solution.py:657
  308.0 1.4 slice_reduce_fusion
  309.4 12.7 %convert_element_type.6 = f32[1536,3072]{1,0:T(8,128)} convert(bf16[1536,3072]{1,0:T(8,128)(2,1)} %get-tuple-element.12) | non-fusion elementwise | flops 4718592 | bytes 28311552 | tf_op jit(solution)/shard_map/convert_element_type | solution.py:693
  322.2 0.0 copy-start.1
  322.2 0.0 copy-start
  322.2 13.3 %convert_element_type.7 = f32[3072,1536]{1,0:T(8,128)} convert(bf16[3072,1536]{1,0:T(8,128)(2,1)} %get-tuple-element.13) | non-fusion elementwise | flops 4718592 | bytes 28311552 | tf_op jit(solution)/shard_map/convert_element_type | solution.py:693
  335.5 0.0 copy-done.1
  335.5 0.8 copy.12
  336.3 0.0 copy-done
  336.3 0.8 copy.13
Async XLA Ops:
  322.2 13.3 %copy-start.1 = (bf16[192,1536]{1,0:T(8,128)(2,1)S(1)}, bf16[192,1536]{1,0:T(8,128)(2,1)}, u32[]{:S(2)}) copy-start(bf16[192,1536]{1,0:T(8,128)(2,1)} %get-tuple-element.20) | copy-start | bytes 1769476
  322.2 14.1 %copy-start = (bf16[192,1536]{1,0:T(8,128)(2,1)S(1)}, bf16[192,1536]{1,0:T(8,128)(2,1)}, u32[]{:S(2)}) copy-start(bf16[192,1536]{1,0:T(8,128)(2,1)} %get-tuple-element.21) | copy-start | bytes 1769476
